TPU v7x, 32 devices: a whole 2x2x4 slice. The times are simulated.
32 devices in a mesh: rows: 32 (over z, y, x, core).
Axes of the slice: x: 2, y: 2, z: 4, core: 2. Of those that a mesh axis runs over, the one named last changes fastest.
Arguments:
- points: float32 [8, 262144], P(None, 'rows'), may hold values from -6 to 6
- inv_scales: float32 [8], replicated, may hold values from 0.25 to 0.8
- pivots: int32 [3, 256], replicated, may hold values from 0 to 262143, as said below
Outputs:
- factor: float32 [262144, 768], P('rows')
- residual: float32 [262144], P('rows')
Inputs may be any that keep to these rules, and one draw needn't show every extreme that they name: `pivots`: each entry is a point index (column of points); all 768 entries are distinct. In each panel at most 32 entries lie among one device's points (indices d * 8192 to (d + 1) * 8192 - 1), and in every panel some device holds exactly 32.
All inputs are finite; a program needn't handle non-finite values.
Results may differ from a plain program's by a relative error of at most 0.0003.
Values sent between devices are 32-bit elements; how exact they have to be, the bound alone decides.
No kernel may reach another device: no remote copies, remote signals or barrier semaphores. Data moves between devices by JAX's collectives and lax.ppermute only.
A program may use at most 192 MiB of HBM per device.

v0:
```python
import jax
import jax.numpy as jnp
from jax import lax
from jax.sharding import PartitionSpec as P

nugget = 0.1


def kernel_tile(left_pts, right_pts, scales):
    left_scaled = left_pts * scales[:, None]
    right_scaled = right_pts * scales[:, None]
    inner_prod = lax.dot_general(
        left_scaled,
        right_scaled,
        (((0,), (0,)), ((), ())),
        precision=lax.Precision.HIGHEST,
        preferred_element_type=jnp.float32,
    )
    squared = (
        jnp.sum(left_scaled * left_scaled, axis=0)[:, None]
        + jnp.sum(right_scaled * right_scaled, axis=0)[None, :]
        - 2.0 * inner_prod
    )
    return jnp.exp(-0.5 * squared)


def slot_layout(pivot_index, row_count, slot_count, my_index):
    pivot_count = pivot_index.shape[0]
    owners = pivot_index // row_count
    local_rows = pivot_index - owners * row_count
    is_mine = owners == my_index
    position = jnp.arange(pivot_count, dtype=jnp.int32)
    same_owner = owners[:, None] == owners[None, :]
    slot_rank = jnp.sum(
        jnp.where(same_owner & (position[None, :] < position[:, None]), 1, 0), axis=1
    ).astype(jnp.int32)
    slot_ids = jnp.arange(slot_count, dtype=jnp.int32)
    chosen = is_mine[None, :] & (slot_rank[None, :] == slot_ids[:, None])
    slot_rows = jnp.sum(jnp.where(chosen, local_rows[None, :], 0), axis=1)
    return (owners, local_rows, is_mine, slot_rank, slot_rows)


def on_device(points, inv_scales, pivots):
    row_count = points.shape[1]
    panel_total = pivots.shape[0]
    pivot_count = pivots.shape[1]
    device_count = lax.axis_size("rows")
    slot_count = 4 * pivot_count // device_count
    my_index = lax.axis_index("rows")
    identity = jnp.eye(pivot_count, dtype=jnp.float32)
    residual = jnp.ones((row_count,), jnp.float32)
    factor_parts = []
    kept_points = []
    kept_factor = []
    kept_inverse = []
    for which_panel in range(panel_total):
        pivot_index = pivots[which_panel]
        earlier = jnp.concatenate(factor_parts, axis=1) if factor_parts else None
        owners, local_rows, is_mine, slot_rank, slot_rows = slot_layout(
            pivot_index, row_count, slot_count, my_index
        )
        slot_place = owners * slot_count + slot_rank
        sent_points = points[:, slot_rows].T
        if earlier is None:
            gathered_points = lax.all_gather(sent_points, "rows", axis=0, tiled=True)
            piv_points = gathered_points[slot_place].T
        else:
            gathered_points, gathered_factor = (
                lax.all_gather(sent_points, "rows", axis=0, tiled=True),
                lax.all_gather(earlier[slot_rows], "rows", axis=0, tiled=True),
            )
            piv_points = gathered_points[slot_place].T
            piv_factor = gathered_factor[slot_place]
        kernel_cols = kernel_tile(points, piv_points, inv_scales)
        pivot_block = kernel_tile(piv_points, piv_points, inv_scales)
        if earlier is not None:
            kernel_cols = kernel_cols - jnp.dot(
                earlier,
                piv_factor.T,
                precision=lax.Precision.HIGHEST,
                preferred_element_type=jnp.float32,
            )
            pivot_block = pivot_block - jnp.dot(
                piv_factor,
                piv_factor.T,
                precision=lax.Precision.HIGHEST,
                preferred_element_type=jnp.float32,
            )
        pivot_block = pivot_block + nugget * identity
        lower_factor = jnp.linalg.cholesky(pivot_block)
        inverse = jax.scipy.linalg.solve_triangular(lower_factor, identity, lower=True)
        kept_points.append(piv_points)
        kept_factor.append(piv_factor if earlier is not None else None)
        kept_inverse.append(inverse)
        new_columns = jnp.dot(
            kernel_cols,
            inverse.T,
            precision=lax.Precision.HIGHEST,
            preferred_element_type=jnp.float32,
        )
        residual = residual - jnp.sum(new_columns * new_columns, axis=1)
        factor_parts.append(new_columns)
    return (jnp.concatenate(factor_parts, axis=1), residual)


def solution(mesh):
    return jax.shard_map(
        on_device,
        mesh=mesh,
        in_specs=(P(None, "rows"), P(), P()),
        out_specs=(P("rows", None), P("rows")),
        check_vma=False,
    )
```

profile of v0, /device:TPU:0, one launch (start us, length us, event | category | flops | bytes accessed | tf_op | source)
XLA Modules:
  0.0 636.9 jit_solution(5612797847553850042)
XLA Ops:
  10.5 3.6 copy.56
  14.1 2.8 gather_fusion.2
  16.9 43.6 %all-gather.3 = f32[32,32,8]{1,2,0:T(8,128)S(1)} all-gather(f32[1,32,8]{1,2,0:T(8,128)S(1)} %copy.63), channel_id=1, replica_groups=mesh['rows'=32] {'rows'}, dimensions={0}, use_global_device_ids=true | all-gather | bytes 33792 | tf_op jit(solution)/shard_map/all_gather | solution.py:69
  60.8 2.8 gather_fusion.6
  63.7 37.0 %all-gather.4 = f32[32,32,8]{1,2,0:T(8,128)S(1)} all-gather(f32[1,32,8]{1,2,0:T(8,128)S(1)} %copy.71), channel_id=1, replica_groups=mesh['rows'=32] {'rows'}, dimensions={0}, use_global_device_ids=true | all-gather | bytes 33792 | tf_op jit(solution)/shard_map/all_gather | solution.py:69
  101.0 2.8 gather_fusion
  103.8 38.3 %all-gather.2 = f32[32,32,8]{1,2,0:T(8,128)S(1)} all-gather(f32[1,32,8]{1,2,0:T(8,128)S(1)} %copy.57), channel_id=1, replica_groups=mesh['rows'=32] {'rows'}, dimensions={0}, use_global_device_ids=true | all-gather | bytes 33792 | tf_op jit(solution)/shard_map/all_gather | solution.py:65
  146.5 11.7 %cholesky.172 = f32[128,128]{1,0:T(8,128)S(1)} custom-call(f32[128,128]{1,0:T(8,128)S(1)} %cholesky.270), custom_call_target="Cholesky" | custom-call | tf_op jit(solution)/shard_map/jit(cholesky)/cholesky | solution.py:90
  158.2 9.8 %custom-call.15 = f32[1,128,128]{1,2,0:T(8,128)S(1)} custom-call(f32[1,128,128]{2,1,0:T(8,128)S(1)} %get-tuple-element.85), custom_call_target="InvertDiagBlocksLowerTriangular" | custom-call | tf_op jit(solution)/shard_map/jit(cholesky)/cholesky | solution.py:90
  168.5 11.7 %cholesky.189 = f32[128,128]{1,0:T(8,128)S(1)} custom-call(f32[128,128]{1,0:T(8,128)S(1)} %convolution_subtract_fusion.7), custom_call_target="Cholesky" | custom-call | tf_op jit(solution)/shard_map/jit(cholesky)/cholesky | solution.py:90
  183.1 4.5 while.6
  184.1 1.4 bitcast_dynamic-update-slice_fusion.6
  186.1 1.4 bitcast_dynamic-update-slice_fusion.6
  187.6 19.7 %custom-call.16 = f32[2,128,128]{1,2,0:T(8,128)S(1)} custom-call(f32[2,128,128]{2,1,0:T(8,128)S(1)} %get-tuple-element.24), custom_call_target="InvertDiagBlocksLowerTriangular" | custom-call | tf_op jit(solution)/shard_map/jit(_solve_triangular)/triangular_solve | solution.py:91
  208.3 10.2 %fusion.8 = f32[8192,256]{1,0:T(8,128)S(1)} fusion(f32[256]{0:T(256)S(1)} %get-tuple-element.37, f32[8192]{0:T(1024)S(1)} %multiply_reduce_fusion.3, f32[8,8192]{1,0:T(8,128)S(1)} %copy-done.1, f32[8]{0:T(128)S(1)} %copy-done.2, f32[256,8]{1,0:T(8,128)S(1)} %gather_fusion.1), kind=kOutput, calls=%fused_computation.30 | convolution fusion | flops 209782784 | bytes 8692768 | tf_op jit(solution)/shard_map/dot_general | solution.py:12
  218.5 10.3 %multiply_reduce_fusion.2 = (f32[8192]{0:T(1024)S(1)}, f32[8192,256]{0,1:T(8,128)}) fusion(f32[8192,256]{1,0:T(8,128)S(1)} %fusion.8, f32[128,256]{1,0:T(8,128)S(1)} %fusion.69, f32[128,256]{1,0:T(8,128)S(1)} %fusion.52), kind=kOutput, calls=%fused_computation.34 | convolution fusion | flops 6446702592 | bytes 17072128 | tf_op jit(solution)/shard_map/dot_general | solution.py:95
  228.7 9.0 %copy.65 = f32[8192,256]{1,0:T(8,128)} copy(f32[8192,256]{0,1:T(8,128)} %get-tuple-element.110) | data formatting | bytes 16777216 | tf_op jit(solution)/shard_map/dot_general | solution.py:95
  237.7 4.6 gather_fusion.4
  242.8 11.7 %fusion.5 = f32[8192,256]{1,0:T(8,128)} fusion(f32[256]{0:T(256)S(1)} %get-tuple-element.36, f32[8192]{0:T(1024)S(1)} %multiply_reduce_fusion.3, f32[8,8192]{1,0:T(8,128)S(1)} %copy-done.1, f32[8]{0:T(128)S(1)} %copy-done.2, f32[256,8]{1,0:T(8,128)S(1)} %gather_fusion.3), kind=kOutput, calls=%fused_computation.26 | convolution fusion | flops 209782784 | bytes 8692768 | tf_op jit(solution)/shard_map/dot_general | solution.py:12
  254.5 37.8 %all-gather.8.cloned.1.call-done = f32[1024,256]{1,0:T(8,128)} async-done(((f32[32,256]{1,0:T(8,128)}), f32[1024,256]{1,0:T(8,128)}) %all-gather.8.cloned.1.call-update) | async-done | bytes 1048592 | tf_op jit(solution)/shard_map/all_gather | solution.py:70
  292.3 2.2 gather_fusion.5
  295.1 11.7 %cholesky.206 = f32[128,128]{1,0:T(8,128)S(1)} custom-call(f32[128,128]{1,0:T(8,128)S(1)} %cholesky.273), custom_call_target="Cholesky" | custom-call | tf_op jit(solution)/shard_map/jit(cholesky)/cholesky | solution.py:90
  306.9 9.8 %custom-call.17 = f32[1,128,128]{1,2,0:T(8,128)S(1)} custom-call(f32[1,128,128]{2,1,0:T(8,128)S(1)} %get-tuple-element.81), custom_call_target="InvertDiagBlocksLowerTriangular" | custom-call | tf_op jit(solution)/shard_map/jit(cholesky)/cholesky | solution.py:90
  317.2 11.7 %cholesky.223 = f32[128,128]{1,0:T(8,128)S(1)} custom-call(f32[128,128]{1,0:T(8,128)S(1)} %convolution_subtract_fusion.6), custom_call_target="Cholesky" | custom-call | tf_op jit(solution)/shard_map/jit(cholesky)/cholesky | solution.py:90
  331.5 3.8 while.7
  332.1 1.3 bitcast_dynamic-update-slice_fusion.7
  334.0 1.3 bitcast_dynamic-update-slice_fusion.7
  335.3 20.1 %custom-call.18 = f32[2,128,128]{1,2,0:T(8,128)S(1)} custom-call(f32[2,128,128]{2,1,0:T(8,128)S(1)} %get-tuple-element.25), custom_call_target="InvertDiagBlocksLowerTriangular" | custom-call | tf_op jit(solution)/shard_map/jit(_solve_triangular)/triangular_solve | solution.py:91
  356.4 17.3 %convolution_subtract_fusion = f32[8192,256]{1,0:T(8,128)S(1)} fusion(f32[8192,256]{1,0:T(8,128)} %fusion.5, f32[8192,256]{0,1:T(8,128)} %get-tuple-element.110, f32[256,256]{1,0:T(8,128)S(1)} %gather_fusion.5), kind=kOutput, calls=%fused_computation.22 | convolution fusion | flops 6444548096 | bytes 25427968 | tf_op jit(solution)/shard_map/dot_general | solution.py:77
  373.7 8.0 %multiply_reduce_fusion.1 = (f32[8192]{0:T(1024)S(1)}, f32[8192,256]{0,1:T(8,128)S(1)}) fusion(f32[8192,256]{1,0:T(8,128)S(1)} %convolution_subtract_fusion, f32[128,256]{1,0:T(8,128)S(1)} %fusion.65, f32[128,256]{1,0:T(8,128)S(1)} %fusion.50), kind=kOutput, calls=%fused_computation.33 | convolution fusion | flops 6446702592 | bytes 17072128 | tf_op jit(solution)/shard_map/dot_general | solution.py:95
  381.8 3.2 copy-done
  385.0 6.4 %pad_maximum_fusion.1 = f32[8192,512]{0,1:T(8,128)} fusion(f32[8192,256]{0,1:T(8,128)S(1)} %get-tuple-element.108, f32[8192,256]{0,1:T(8,128)S(1)} %bitcast.167), kind=kLoop, calls=%fused_computation.17 | loop fusion | flops 4194304 | bytes 33554432 | tf_op jit(solution)/shard_map/concatenate | solution.py:58
  391.4 17.5 %copy.73 = f32[8192,512]{1,0:T(8,128)} copy(f32[8192,512]{0,1:T(8,128)} %pad_maximum_fusion.1) | data formatting | bytes 33554432 | tf_op jit(solution)/shard_map/concatenate | solution.py:58
  408.9 7.0 %gather_fusion.8 = f32[32,512]{1,0:T(8,128)} fusion(f32[8192,512]{1,0:T(8,128)} %copy.73, s32[1024]{0:T(1024)S(1)} %pad_clamp_fusion.1), kind=kCustom, calls=%fused_computation.8 | custom fusion | bytes 131200 | tf_op jit(solution)/shard_map/gather | solution.py:70
  415.9 55.5 %all-gather.10.cloned.1.call-done = f32[1024,512]{1,0:T(8,128)} async-done(((f32[32,512]{1,0:T(8,128)}), f32[1024,512]{1,0:T(8,128)}) %all-gather.10.cloned.1.call-update) | async-done | bytes 2097168 | tf_op jit(solution)/shard_map/all_gather | solution.py:70
  471.4 2.8 gather_fusion.9
  474.8 32.5 %fusion.90 = f32[8192,256]{1,0:T(8,128)} fusion(f32[256,512]{1,0:T(8,128)S(1)} %gather_fusion.9, f32[8192,256]{0,1:T(8,128)} %copy-done, f32[8192,256]{0,1:T(8,128)} %get-tuple-element.110), kind=kOutput, calls=%fused_computation.235 | convolution fusion | flops 12889096192 | bytes 25690112 | tf_op jit(solution)/shard_map/dot_general | solution.py:77
  507.9 11.7 %cholesky.240 = f32[128,128]{1,0:T(8,128)S(1)} custom-call(f32[128,128]{1,0:T(8,128)S(1)} %cholesky.276), custom_call_target="Cholesky" | custom-call | tf_op jit(solution)/shard_map/jit(cholesky)/cholesky | solution.py:90
  519.7 9.8 %custom-call.19 = f32[1,128,128]{1,2,0:T(8,128)S(1)} custom-call(f32[1,128,128]{2,1,0:T(8,128)S(1)} %get-tuple-element.77), custom_call_target="InvertDiagBlocksLowerTriangular" | custom-call | tf_op jit(solution)/shard_map/jit(cholesky)/cholesky | solution.py:90
  530.0 11.7 %cholesky.257 = f32[128,128]{1,0:T(8,128)S(1)} custom-call(f32[128,128]{1,0:T(8,128)S(1)} %convolution_subtract_fusion.5), custom_call_target="Cholesky" | custom-call | tf_op jit(solution)/shard_map/jit(cholesky)/cholesky | solution.py:90
  544.5 4.1 while.8
  545.1 1.4 bitcast_dynamic-update-slice_fusion.8
  547.2 1.4 bitcast_dynamic-update-slice_fusion.8
  548.6 19.8 %custom-call.20 = f32[2,128,128]{1,2,0:T(8,128)S(1)} custom-call(f32[2,128,128]{2,1,0:T(8,128)S(1)} %get-tuple-element.26), custom_call_target="InvertDiagBlocksLowerTriangular" | custom-call | tf_op jit(solution)/shard_map/jit(_solve_triangular)/triangular_solve | solution.py:91
  569.5 12.7 %fusion.9 = f32[8192,256]{1,0:T(8,128)S(1)} fusion(f32[8192,256]{1,0:T(8,128)} %fusion.90, f32[256]{0:T(256)S(1)} %get-tuple-element.35, f32[8192]{0:T(1024)S(1)} %multiply_reduce_fusion.3, f32[8,8192]{1,0:T(8,128)S(1)} %copy-done.1, f32[8]{0:T(128)S(1)} %copy-done.2, f32[256,8]{1,0:T(8,128)S(1)} %gather_fusion.7), kind=kOutput, calls=%fused_computation.31 | convolution fusion | flops 211879936 | bytes 17081376 | tf_op jit(solution)/shard_map/dot_general | solution.py:12
  582.3 10.4 %multiply_reduce_fusion = (f32[8192]{0:T(1024)S(1)}, f32[8192,256]{0,1:T(8,128)}) fusion(f32[8192,256]{1,0:T(8,128)S(1)} %fusion.9, f32[128,256]{1,0:T(8,128)S(1)} %fusion.61, f32[128,256]{1,0:T(8,128)S(1)} %fusion.48), kind=kOutput, calls=%fused_computation.32 | convolution fusion | flops 6446702592 | bytes 17072128 | tf_op jit(solution)/shard_map/dot_general | solution.py:95
  592.6 11.9 %pad_maximum_fusion = f32[8192,768]{0,1:T(8,128)} fusion(f32[8192,256]{0,1:T(8,128)} %get-tuple-element.106, f32[8192,256]{0,1:T(8,128)S(1)} %bitcast.171, f32[8192,256]{0,1:T(8,128)S(1)} %bitcast.169), kind=kLoop, calls=%fused_computation.16 | loop fusion | flops 12582912 | bytes 50331648 | tf_op jit(solution)/shard_map/concatenate | solution.py:103
  604.5 24.7 %copy.78 = f32[8192,768]{1,0:T(8,128)} copy(f32[8192,768]{0,1:T(8,128)} %pad_maximum_fusion) | data formatting | bytes 50331648
  (121 shorter events, 23.8 us)
Async XLA Ops:
  7.2 138.5 %copy-start.2 = (f32[8]{0:T(128)S(1)}, f32[8]{0:T(128)}, u32[]{:S(2)}) copy-start(f32[8]{0:T(128)} %param.7) | copy-start | bytes 100
  7.2 285.1 %all-gather.8.cloned.1.call-start = ((), (), s32[]{:S(2)}) async-start(), calls=%async_computation | async-start | bytes 1081344 | tf_op jit(solution)/shard_map/all_gather | solution.py:70
  10.5 197.8 %copy-start.1 = (f32[8,8192]{1,0:T(8,128)S(1)}, f32[8,8192]{1,0:T(8,128)}, u32[]{:S(2)}) copy-start(f32[8,8192]{1,0:T(8,128)} %param.6) | copy-start | bytes 786436
  242.4 229.0 %all-gather.10.cloned.1.call-start = ((), (), s32[]{:S(2)}) async-start(), calls=%async_computation.1 | async-start | bytes 2162688 | tf_op jit(solution)/shard_map/all_gather | solution.py:70
  355.4 29.6 %slice-start = ((s8[8388608]{0:T(1024)(128)(4,1)}), s8[4194304]{0:T(1024)(128)(4,1)S(1)}, s32[]{:S(2)}) async-start(s8[8388608]{0:T(1024)(128)(4,1)} %bitcast.166), calls=%async_computation.2 | async-start | bytes 8388608
  356.4 28.5 %slice-start.1 = ((s8[8388608]{0:T(1024)(128)(4,1)}), s8[4194304]{0:T(1024)(128)(4,1)S(1)}, s32[]{:S(2)}) async-start(s8[8388608]{0:T(1024)(128)(4,1)} %bitcast.166), calls=%async_computation.3 | async-start | bytes 8388608
  381.8 3.2 copy-start
  569.5 23.1 %slice-start.2 = ((s8[8388608]{0:T(1024)(128)(4,1)}), s8[4194304]{0:T(1024)(128)(4,1)S(1)}, s32[]{:S(2)}) async-start(s8[8388608]{0:T(1024)(128)(4,1)} %bitcast.168), calls=%async_computation.4 | async-start | bytes 8388608
  569.5 23.1 %slice-start.4 = ((s8[8388608]{0:T(1024)(128)(4,1)}), s8[4194304]{0:T(1024)(128)(4,1)S(1)}, s32[]{:S(2)}) async-start(s8[8388608]{0:T(1024)(128)(4,1)} %bitcast.170), calls=%async_computation.6 | async-start | bytes 8388608
  582.2 10.4 %slice-start.3 = ((s8[8388608]{0:T(1024)(128)(4,1)}), s8[4194304]{0:T(1024)(128)(4,1)S(1)}, s32[]{:S(2)}) async-start(s8[8388608]{0:T(1024)(128)(4,1)} %bitcast.168), calls=%async_computation.5 | async-start | bytes 8388608
  582.2 10.4 %slice-start.5 = ((s8[8388608]{0:T(1024)(128)(4,1)}), s8[4194304]{0:T(1024)(128)(4,1)S(1)}, s32[]{:S(2)}) async-start(s8[8388608]{0:T(1024)(128)(4,1)} %bitcast.170), calls=%async_computation.7 | async-start | bytes 8388608
Sparse Core Ops, SparseCore 0:
  242.5 49.7 all-gather.7
  416.0 55.3 all-gather.9
where the time goes:
time: 648 us; the launch traced here: 637 us
  other arithmetic  187 us (29%)
  matrix products  120 us (19%)
  blocking collectives  119 us (18%)
  local copies, waits for them, and re-layouts  98.3 us (15%)
  waiting for transfers between devices  93.3 us (14%)
  between operations  18.8 us (3%)
    another operation x21, other arithmetic, on_device(): lower_factor = jnp.linalg.cholesky(pivot_block)  104 us
    all_gather x2, waiting for transfers between devices, on_device(): lax.all_gather(earlier[slot_rows], 'rows', axis=0, tiled=True)  93.3 us
    all_gather x2, blocking collectives, on_device(): lax.all_gather(sent_points, 'rows', axis=0, tiled=True)  80.5 us
    another operation x7, other arithmetic, on_device(): jax.scipy.linalg.solve_triangular(lower_factor, identity, lower=True)  59.7 us
    dot_general x2, matrix products, on_device(): jnp.dot(earlier, piv_factor.T, precision=lax.Precision.HIGHEST, preferred...  49.7 us
    all_gather x1, blocking collectives, on_device(): gathered_points = lax.all_gather(sent_points, 'rows', axis=0, tiled=True)  38.3 us
    dot_general x6, matrix products, kernel_tile(): lax.dot_general(left_scaled, right_scaled, (((0,), (0,)), ((), ())), prec...  35.9 us
    unnamed x23, local copies, waits for them, and re-layouts  31.7 us
  transfers between devices with their start and end apart: 2, of which 2 were waited for; matrix products, arithmetic and copies ran while one was open for 2% of the time, Pallas kernels for 0%

commit v1 on v0

v1 whole, which is shorter than its diff:
```python
import functools

import jax
import jax.numpy as jnp
from jax import lax
from jax.experimental import pallas as pl
from jax.experimental.pallas import tpu as pltpu
from jax.sharding import PartitionSpec as P

nugget = 0.1
exp2_scale = 1.2011224087864498
group = 8
lanes = 128
block = 128
feature_rows = 64
high = lax.Precision.HIGHEST


def product(a, b, a_dim=1, b_dim=0, precision=None):
    return lax.dot_general(
        a,
        b,
        (((a_dim,), (b_dim,)), ((), ())),
        precision=precision,
        preferred_element_type=jnp.float32,
    )


def iota(shape, dim):
    return lax.broadcasted_iota(jnp.int32, shape, dim)


def widen(x):
    return x.astype(jnp.float32)


def narrow(x):
    return x.astype(jnp.bfloat16)


def select_kernel(row_count, slot_count, device_count, points_ref, pivots_ref, send_ref, place_ref):
    panels, pivot_count = pivots_ref.shape
    me = lax.axis_index("rows")
    before = narrow(
        jnp.where(iota((pivot_count, pivot_count), 0) < iota((pivot_count, pivot_count), 1), 1.0, 0.0)
    )
    chosen_parts = []
    value_parts = []
    for panel in range(panels):
        index = pivots_ref[panel : panel + 1, :]
        owner = lax.div(index, row_count)
        local = index - owner * row_count
        owned = jnp.where(
            iota((device_count, pivot_count), 0) == jnp.broadcast_to(owner, (device_count, pivot_count)), 1.0, 0.0
        )
        counts = product(narrow(owned), before)
        rank = jnp.sum(owned * counts, axis=0, keepdims=True).astype(jnp.int32)
        slot = rank + panel * slot_count
        place_ref[panel : panel + 1, :] = owner * lanes + slot
        mine = jnp.where(owner == me, slot, -1)
        chosen_parts.append(
            jnp.where(iota((lanes, pivot_count), 0) == jnp.broadcast_to(mine, (lanes, pivot_count)), 1.0, 0.0)
        )
        tile = lax.div(local, lanes)
        lane = local - tile * lanes
        which = iota((group, pivot_count), 0)
        value_parts.append(
            jnp.where(which == 0, widen(tile), jnp.where(which == 1, widen(lane), 0.0))
        )
    chosen = narrow(jnp.concatenate(chosen_parts, axis=1))
    values = narrow(jnp.concatenate(value_parts, axis=1))
    found = product(values, chosen, 1, 1).astype(jnp.int32)
    tile = jnp.broadcast_to(found[0:1, :], (group, lanes))
    lane = jnp.broadcast_to(found[1:2, :], (group, lanes))
    taken = jnp.zeros((group, lanes), jnp.float32)
    for t in range(row_count // lanes):
        here = jnp.take_along_axis(points_ref[:, t * lanes : (t + 1) * lanes], lane, axis=1)
        taken = jnp.where(tile == t, here, taken)
    for d in range(device_count):
        send_ref[d] = taken


def scale_column(scales_ref):
    sub = iota((group, 1), 0)
    column = jnp.zeros((group, 1), jnp.float32)
    for d in range(group):
        column = jnp.where(sub == d, scales_ref[d], column)
    return column * exp2_scale


def split3(x):
    top = widen(narrow(x))
    rest = x - top
    mid = widen(narrow(rest))
    return top, mid, widen(narrow(rest - mid))


def features(scaled, left):
    top, mid, low = split3(scaled)
    count = scaled.shape[1]
    norm = split3(jnp.broadcast_to(-0.5 * jnp.sum(scaled * scaled, axis=0, keepdims=True), (group, count)))
    sub = iota((group, count), 0)
    at = 0 if left else 3
    extra = jnp.where(sub < 6, 1.0, 0.0)
    for i in range(3):
        extra = jnp.where(sub == at + i, norm[i], extra)
    zero = jnp.zeros((group, count), jnp.float32)
    if left:
        parts = [top, top, mid, top, low, mid, extra, zero]
    else:
        parts = [top, mid, top, low, top, mid, extra, zero]
    return jnp.concatenate(parts, axis=0)


def factor_block(matrix):
    groups = block // group
    sub = iota((group, block), 0)
    lane = iota((group, block), 1)
    rows = [matrix[g * group : (g + 1) * group, :] for g in range(groups)]
    inv = [jnp.where(lane == sub + g * group, 1.0, 0.0) for g in range(groups)]
    done = []

    def spread(row, at):
        return jnp.broadcast_to(row[at : at + 1, :], (group, block))

    for w in range(groups):
        cols = [
            [
                jnp.broadcast_to(rows[g][:, w * group + k : w * group + k + 1], (group, block))
                for k in range(group)
            ]
            for g in range(w, groups)
        ]
        near = list(cols[0])
        row_s, row_x, forward = rows[w], inv[w], inv[w]
        diag = None
        for j in range(group):
            pivot = spread(near[j], j)
            recip = 1.0 / pivot
            mult = near[j] * recip
            both = jnp.where(sub == j, 1.0 - recip, mult)
            below = jnp.where(sub > j, mult, 0.0)
            diag = pivot if diag is None else jnp.where(sub >= j, pivot, diag)
            row_s = row_s - both * spread(row_s, j)
            row_x = row_x - both * spread(row_x, j)
            if j < group - 1:
                forward = forward - below * spread(forward, j)
            for k in range(j + 1, group):
                near[k] = near[k] - both * spread(near[k], j)
        done.append(forward * lax.rsqrt(diag))
        for g in range(w + 1, groups):
            c = cols[g - w]
            s, x = rows[g], inv[g]
            for k in range(group):
                s = s - c[k] * spread(row_s, k)
                x = x - c[k] * spread(row_x, k)
            rows[g], inv[g] = s, x
    return jnp.concatenate(done, axis=0)


def invert_factor(s_ref, w_ref, blocks):
    at = lambda i: slice(i * block, (i + 1) * block)
    total = blocks * block
    for b in range(blocks):
        x = factor_block(s_ref[at(b), at(b)])
        w_ref[at(b), at(b)] = x
        if b > 0:
            w_ref[at(b), 0 : b * block] = product(x, w_ref[at(b), 0 : b * block], precision=high)
        if b + 1 < blocks:
            w_ref[at(b), (b + 1) * block : total] = jnp.zeros((block, total - (b + 1) * block), jnp.float32)
            y = product(x, s_ref[at(b), (b + 1) * block : total], precision=high)
            for i in range(b + 1, blocks):
                mine = y[:, (i - b - 1) * block : (i - b) * block]
                s_ref[at(i), i * block : total] = s_ref[at(i), i * block : total] - product(
                    mine, y[:, (i - b - 1) * block :], 0, 0, high
                )
            for i in range(b + 1, blocks):
                mine = y[:, (i - b - 1) * block : (i - b) * block]
                t = product(mine, w_ref[at(b), 0 : (b + 1) * block], 0, 0, high)
                if b > 0:
                    w_ref[at(i), 0 : b * block] = w_ref[at(i), 0 : b * block] - t[:, 0 : b * block]
                w_ref[at(i), at(b)] = -t[:, b * block :]


def pivot_kernel(
    device_count, place_ref, got_ref, scales_ref, right_ref, top_ref, low_ref, mean_ref, shift_ref, s_ref, w_ref
):
    panels, pivot_count = place_ref.shape
    total = panels * pivot_count
    parts = []
    for panel in range(panels):
        for half in range(pivot_count // lanes):
            place = place_ref[panel : panel + 1, half * lanes : (half + 1) * lanes]
            owner = jnp.broadcast_to(lax.div(place, lanes), (group, lanes))
            lane = jnp.broadcast_to(place, (group, lanes)) - owner * lanes
            taken = jnp.zeros((group, lanes), jnp.float32)
            for d in range(device_count):
                taken = jnp.where(owner == d, jnp.take_along_axis(got_ref[d], lane, axis=1), taken)
            parts.append(taken)
    scaled = jnp.concatenate(parts, axis=1) * scale_column(scales_ref)
    left = narrow(features(scaled, True))
    right = narrow(features(scaled, False))
    right_ref[...] = right
    kernel = jnp.exp2(product(left, right, 0, 0))
    mean = jnp.sum(kernel, axis=0, keepdims=True) * (1.0 / total)
    mean_ref[...] = jnp.broadcast_to(mean, (group, total))
    s_ref[...] = jnp.where(iota((total, total), 0) == iota((total, total), 1), kernel + nugget, kernel)
    invert_factor(s_ref, w_ref, total // block)
    inverse = w_ref[...]
    top = narrow(inverse)
    top_ref[...] = top
    low_ref[...] = narrow(inverse - widen(top))
    shift_ref[...] = product(jnp.broadcast_to(mean, (group, total)), inverse, 1, 1, high)


def rows_kernel(panel_width, points_ref, scales_ref, right_ref, top_ref, low_ref, mean_ref, shift_ref, out_ref, res_ref):
    total = right_ref.shape[1]
    scaled = points_ref[...] * scale_column(scales_ref)
    left = narrow(features(scaled, True))
    kernel = jnp.exp2(product(left, right_ref[...], 0, 0)) - mean_ref[0:1, :]
    top = narrow(kernel)
    low = narrow(kernel - widen(top))
    squares = None
    for p in range(total // panel_width):
        at = slice(p * panel_width, (p + 1) * panel_width)
        depth = (p + 1) * panel_width
        a = jnp.concatenate([top[:, :depth], low[:, :depth], top[:, :depth]], axis=1)
        b = jnp.concatenate([top_ref[at, :depth], top_ref[at, :depth], low_ref[at, :depth]], axis=1)
        new = product(a, b, 1, 1) + shift_ref[0:1, at]
        out_ref[:, at] = new
        for q in range(panel_width // lanes):
            piece = new[:, q * lanes : (q + 1) * lanes]
            squares = piece * piece if squares is None else squares + piece * piece
    res_ref[...] = 1.0 - jnp.sum(squares.T, axis=0, keepdims=True)


def on_device(points, inv_scales, pivots):
    dim, row_count = points.shape
    panels, pivot_count = pivots.shape
    device_count = lax.axis_size("rows")
    slot_count = 4 * pivot_count // device_count
    total = panels * pivot_count
    assert dim == group and panels * slot_count <= lanes
    f32, bf16 = jnp.float32, jnp.bfloat16
    shape = jax.ShapeDtypeStruct
    vmem = pl.BlockSpec(memory_space=pltpu.VMEM)
    smem = pl.BlockSpec(memory_space=pltpu.SMEM)
    params = pltpu.CompilerParams(vmem_limit_bytes=48 * 2**20)

    send, place = pl.pallas_call(
        functools.partial(select_kernel, row_count, slot_count, device_count),
        out_shape=(shape((device_count, group, lanes), f32), shape((panels, pivot_count), jnp.int32)),
        in_specs=[vmem, vmem],
        out_specs=(vmem, vmem),
        compiler_params=params,
        name="select",
    )(points, pivots)
    got = lax.all_to_all(send, "rows", 0, 0)
    right, top, low, mean, shift = pl.pallas_call(
        functools.partial(pivot_kernel, device_count),
        out_shape=(
            shape((feature_rows, total), bf16),
            shape((total, total), bf16),
            shape((total, total), bf16),
            shape((group, total), f32),
            shape((group, total), f32),
        ),
        in_specs=[vmem, vmem, smem],
        out_specs=(vmem,) * 5,
        scratch_shapes=[pltpu.VMEM((total, total), f32), pltpu.VMEM((total, total), f32)],
        compiler_params=params,
        name="pivots",
    )(place, got, inv_scales)
    tile = 512
    whole = lambda s: pl.BlockSpec(s, lambda i: (0,) * len(s))
    factor, residual = pl.pallas_call(
        functools.partial(rows_kernel, pivot_count),
        grid=(row_count // tile,),
        out_shape=(shape((row_count, total), f32), shape((1, row_count), f32)),
        in_specs=[
            pl.BlockSpec((group, tile), lambda i: (0, i)),
            smem,
            whole((feature_rows, total)),
            whole((total, total)),
            whole((total, total)),
            whole((group, total)),
            whole((group, total)),
        ],
        out_specs=(pl.BlockSpec((tile, total), lambda i: (i, 0)), pl.BlockSpec((1, tile), lambda i: (0, i))),
        compiler_params=params,
        name="rows",
    )(points, inv_scales, right, top, low, mean, shift)
    return factor, residual.reshape(row_count)


def solution(mesh):
    return jax.shard_map(
        on_device,
        mesh=mesh,
        in_specs=(P(None, "rows"), P(), P()),
        out_specs=(P("rows", None), P("rows")),
        check_vma=False,
    )
```

time: 648 us -> 86.9 us (0.13); the launches traced: 637 us -> 86.7 us
  other arithmetic: 187 us -> 0 us
  matrix products: 120 us -> 0 us
  blocking collectives: 119 us -> 15.3 us
  local copies, waits for them, and re-layouts: 98.3 us -> 3.93 us
  waiting for transfers between devices: 93.3 us -> 0 us
  Pallas kernels: 0 us -> 66.7 us
  between operations: 18.8 us -> 0.65 us
    another operation x28 -> x0, other arithmetic: 164 us -> none  [the longest x21 104 us: on_device(): lower_factor = jnp.linalg.cholesky(pivot_block)]
    all_gather x3 -> x0, blocking collectives: 119 us -> none  [the longest x2 80.5 us: on_device(): lax.all_gather(sent_points, 'rows', axis=0, tiled=True)]
    dot_general x13 -> x0, matrix products: 115 us -> none  [the longest x2 49.7 us: on_device(): jnp.dot(earlier, piv_factor.T, precision=lax.Precision.HIGHEST, preferred...]
    all_gather x2 -> x0, waiting for transfers between devices: 93.3 us -> none  [on_device(): lax.all_gather(earlier[slot_rows], 'rows', axis=0, tiled=True)]
    pallas_call x0 -> x3, Pallas kernels: none -> 66.7 us  [the longest x1 36.1 us: on_device(): pl.pallas_call(functools.partial(pivot_kernel, device_count), out_shape=(...]
    unnamed x23 -> x10, local copies, waits for them, and re-layouts: 31.7 us -> 3.93 us
    gather x10 -> x0, local copies, waits for them, and re-layouts: 27.1 us -> none  [the longest x2 11.6 us: on_device(): earlier[slot_rows]]
    concatenate x2 -> x0, other arithmetic: 18.3 us -> none  [the longest x1 11.9 us: on_device(): return (jnp.concatenate(factor_parts, axis=1), residual)]
  transfers between devices with their start and end apart: 2 -> 0, of which waited for: 2 -> 0; matrix products, arithmetic and copies ran while one was open for 2% -> 0% of each run, Pallas kernels for 0% -> 0%
where the time goes in v1:
time: 86.9 us; the launch traced here: 86.7 us
  Pallas kernels  66.7 us (77%)
  blocking collectives  15.3 us (18%)
  local copies, waits for them, and re-layouts  3.93 us (5%)
    pallas_call x1, Pallas kernels, on_device(): pl.pallas_call(functools.partial(pivot_kernel, device_count), out_shape=(...  36.1 us
    pallas_call x1, Pallas kernels, on_device(): pl.pallas_call(functools.partial(rows_kernel, pivot_count), grid=(row_cou...  30.1 us
    all_to_all x1, blocking collectives, on_device(): got = lax.all_to_all(send, 'rows', 0, 0)  15.3 us
    unnamed x10, local copies, waits for them, and re-layouts  3.93 us

profile of v1, /device:TPU:0, one launch (start us, length us, event | category | flops | bytes accessed | tf_op | source)
XLA Modules:
  0.0 86.7 jit_solution(491193211743329426)
XLA Ops:
  0.6 0.0 copy-start
  0.6 0.9 %copy-done = f32[8,8192]{1,0:T(8,128)S(1)} copy-done((f32[8,8192]{1,0:T(8,128)S(1)}, f32[8,8192]{1,0:T(8,128)}, u32[]{:S(2)}) %copy-start) | copy-done | bytes 262168
  1.6 0.0 copy-start.2
  1.6 0.7 copy-done.2
  2.3 0.5 select.1
  2.8 15.3 %all_to_all.5.got_ref = f32[32,8,128]{2,1,0:T(8,128)S(1)} all-to-all(f32[32,8,128]{2,1,0:T(8,128)S(1)} %get-tuple-element.12), channel_id=1, replica_groups=mesh['rows'=32] {'rows'}, dimensions={0} | all-to-all | bytes 262144 | tf_op jit(solution)/shard_map/all_to_all | solution.py:258
  18.1 0.0 copy-start.3
  18.1 0.7 copy-done.3
  18.8 36.1 %pivots.1 = (bf16[64,768]{1,0:T(8,128)(2,1)S(1)}, bf16[768,768]{1,0:T(8,128)(2,1)S(1)}, bf16[768,768]{1,0:T(8,128)(2,1)S(1)}, f32[8,768]{1,0:T(8,128)S(1)}, f32[8,768]{1,0:T(8,128)S(1)}) custom-call(s32[3,256]{1,0:T(4,128)S(1)} %get-tuple-element.11.place_ref, f32[32,8,128]{2,1,0:T(8,128)S(1)} %all_to_all.5.got_ref, f32[8]{0:T(128)S(1)} %copy-done.3), custom_call_target="tpu_custom_call" | custom-call | tf_op jit(solution)/shard_map/pivots/pallas_call | solution.py:259
  54.9 0.0 copy-start.1
  54.9 1.0 %copy-done.1 = f32[8,8192]{1,0:T(8,128)S(1)} copy-done((f32[8,8192]{1,0:T(8,128)S(1)}, f32[8,8192]{1,0:T(8,128)}, u32[]{:S(2)}) %copy-start.1) | copy-done | bytes 262168
  55.9 0.0 copy-start.4
  55.9 0.7 copy-done.4
  56.5 30.1 %rows.1 = (f32[8192,768]{1,0:T(8,128)}, f32[1,8192]{1,0:T(1,128)}) custom-call(f32[8,8192]{1,0:T(8,128)S(1)} %copy-done.1, f32[8]{0:T(128)S(1)} %copy-done.4, bf16[64,768]{1,0:T(8,128)(2,1)S(1)} %get-tuple-element.13.right_ref, bf16[768,768]{1,0:T(8,128)(2,1)S(1)} %get-tuple-element.14.top_ref, bf16[768,768]{1,0:T(8,128)(2,1)S(1)} %get-tuple-element.15.low_ref, ...), custom_call_target="tpu_custom_call" | custom-call | tf_op jit(solution)/shard_map/rows/pallas_call | solution.py:276
Async XLA Ops:
  0.6 1.0 %copy-start = (f32[8,8192]{1,0:T(8,128)S(1)}, f32[8,8192]{1,0:T(8,128)}, u32[]{:S(2)}) copy-start(f32[8,8192]{1,0:T(8,128)} %points_ref.3) | copy-start | bytes 786436
  1.6 0.7 copy-start.2
  18.1 0.7 copy-start.3
  54.9 1.0 %copy-start.1 = (f32[8,8192]{1,0:T(8,128)S(1)}, f32[8,8192]{1,0:T(8,128)}, u32[]{:S(2)}) copy-start(f32[8,8192]{1,0:T(8,128)} %points_ref.3) | copy-start | bytes 786436
  55.9 0.7 copy-start.4

commit v2 on v1

v2 whole, which is shorter than its diff:
```python
import functools

import jax
import jax.numpy as jnp
from jax import lax
from jax.experimental import pallas as pl
from jax.experimental.pallas import tpu as pltpu
from jax.sharding import PartitionSpec as P

nugget = 0.1
exp2_scale = 1.2011224087864498
group = 8
lanes = 128
block = 128
window = 16
feature_rows = 64
high = lax.Precision.HIGHEST


def product(a, b, a_dim=1, b_dim=0, precision=None):
    return lax.dot_general(
        a,
        b,
        (((a_dim,), (b_dim,)), ((), ())),
        precision=precision,
        preferred_element_type=jnp.float32,
    )


def iota(shape, dim):
    return lax.broadcasted_iota(jnp.int32, shape, dim)


def widen(x):
    return x.astype(jnp.float32)


def narrow(x):
    return x.astype(jnp.bfloat16)


def select_kernel(row_count, slot_count, device_count, points_ref, pivots_ref, send_ref, place_ref):
    panels, pivot_count = pivots_ref.shape
    me = lax.axis_index("rows")
    before = narrow(
        jnp.where(iota((pivot_count, pivot_count), 0) < iota((pivot_count, pivot_count), 1), 1.0, 0.0)
    )
    chosen_parts = []
    value_parts = []
    for panel in range(panels):
        index = pivots_ref[panel : panel + 1, :]
        owner = lax.div(index, row_count)
        local = index - owner * row_count
        owned = jnp.where(
            iota((device_count, pivot_count), 0) == jnp.broadcast_to(owner, (device_count, pivot_count)), 1.0, 0.0
        )
        counts = product(narrow(owned), before)
        rank = jnp.sum(owned * counts, axis=0, keepdims=True).astype(jnp.int32)
        slot = rank + panel * slot_count
        place_ref[panel : panel + 1, :] = owner * lanes + slot
        mine = jnp.where(owner == me, slot, -1)
        chosen_parts.append(
            jnp.where(iota((lanes, pivot_count), 0) == jnp.broadcast_to(mine, (lanes, pivot_count)), 1.0, 0.0)
        )
        tile = lax.div(local, lanes)
        lane = local - tile * lanes
        which = iota((group, pivot_count), 0)
        value_parts.append(
            jnp.where(which == 0, widen(tile), jnp.where(which == 1, widen(lane), 0.0))
        )
    chosen = narrow(jnp.concatenate(chosen_parts, axis=1))
    values = narrow(jnp.concatenate(value_parts, axis=1))
    found = product(values, chosen, 1, 1).astype(jnp.int32)
    tile = jnp.broadcast_to(found[0:1, :], (group, lanes))
    lane = jnp.broadcast_to(found[1:2, :], (group, lanes))
    taken = jnp.zeros((group, lanes), jnp.float32)
    for t in range(row_count // lanes):
        here = jnp.take_along_axis(points_ref[:, t * lanes : (t + 1) * lanes], lane, axis=1)
        taken = jnp.where(tile == t, here, taken)
    for d in range(device_count):
        send_ref[d] = taken


def scale_column(scales_ref):
    sub = iota((group, 1), 0)
    column = jnp.zeros((group, 1), jnp.float32)
    for d in range(group):
        column = jnp.where(sub == d, scales_ref[d], column)
    return column * exp2_scale


def split3(x):
    top = widen(narrow(x))
    rest = x - top
    mid = widen(narrow(rest))
    return top, mid, widen(narrow(rest - mid))


def features(scaled, left):
    top, mid, low = split3(scaled)
    count = scaled.shape[1]
    norm = split3(jnp.broadcast_to(-0.5 * jnp.sum(scaled * scaled, axis=0, keepdims=True), (group, count)))
    sub = iota((group, count), 0)
    at = 0 if left else 3
    extra = jnp.where(sub < 6, 1.0, 0.0)
    for i in range(3):
        extra = jnp.where(sub == at + i, norm[i], extra)
    zero = jnp.zeros((group, count), jnp.float32)
    if left:
        parts = [top, top, mid, top, low, mid, extra, zero]
    else:
        parts = [top, mid, top, low, top, mid, extra, zero]
    return jnp.concatenate(parts, axis=0)


def spread(row, at):
    return jnp.broadcast_to(row[at : at + 1, :], row.shape)


def column(rows, at):
    return jnp.broadcast_to(rows[:, at : at + 1], rows.shape)


def tree_sum(terms):
    while len(terms) > 1:
        terms = [sum(terms[i : i + 2][1:], terms[i]) for i in range(0, len(terms), 2)]
    return terms[0]


def stack_left(x):
    top, mid, low = split3(x)
    return jnp.concatenate([top, top, mid, top, low, mid], axis=0)


def stack_right(x):
    top, mid, low = split3(x)
    return narrow(jnp.concatenate([top, mid, top, low, top, mid], axis=0))


def factor_block(matrix, answer):
    windows = block // window
    sub = iota((window, block), 0)
    lane = iota((window, block), 1)
    rows = [matrix[w * window : (w + 1) * window, :] for w in range(windows)]
    inv = [jnp.where(lane == sub + w * window, 1.0, 0.0) for w in range(windows)]
    for w in range(windows):
        first = w * window
        near = [column(rows[w], first + k) for k in range(window)]
        after = [column(rows[w + 1], first + k) for k in range(window)] if w + 1 < windows else []
        if w + 2 < windows:
            left = narrow(stack_left(rows[w]).T)[(w + 2) * window :, :]
        row_s, row_x, forward = rows[w], inv[w], inv[w]
        diag = None
        for j in range(0, window, 2):
            a, b, c = spread(near[j], j), spread(near[j + 1], j), spread(near[j + 1], j + 1)
            recip = 1.0 / (a * c - b * b)
            n1 = near[j] - jnp.where(sub == j, 1.0, 0.0)
            n2 = near[j + 1] - jnp.where(sub == j + 1, 1.0, 0.0)
            m1 = (n1 * c - n2 * b) * recip
            m2 = (n2 * a - n1 * b) * recip
            for k in range(j + 2, window):
                near[k] = near[k] - (m1 * spread(near[k], j) + m2 * spread(near[k], j + 1))
            over = 1.0 / a
            f1 = jnp.where(sub > j, near[j] * over, 0.0)
            f2 = jnp.where(sub > j + 1, (near[j + 1] - near[j] * (b * over)) * (a * recip), 0.0)
            diag = a if diag is None else jnp.where(sub >= j, a, diag)
            diag = jnp.where(sub >= j + 1, c - b * (b * over), diag)
            row_s = row_s - (m1 * spread(row_s, j) + m2 * spread(row_s, j + 1))
            row_x = row_x - (m1 * spread(row_x, j) + m2 * spread(row_x, j + 1))
            forward = forward - f1 * spread(forward, j)
            if j + 2 < window:
                forward = forward - f2 * spread(forward, j + 1)
        answer.append(forward * lax.rsqrt(diag))
        if w + 1 < windows:
            rows[w + 1] = rows[w + 1] - tree_sum([after[k] * spread(row_s, k) for k in range(window)])
            inv[w + 1] = inv[w + 1] - tree_sum([after[k] * spread(row_x, k) for k in range(window)])
        if w + 2 < windows:
            change = product(left, stack_right(jnp.concatenate([row_s, row_x], axis=1)))
            for v in range(w + 2, windows):
                at = (v - w - 2) * window
                rows[v] = rows[v] - change[at : at + window, :block]
                inv[v] = inv[v] - change[at : at + window, block:]
        yield w


def two_parts(x):
    top = narrow(x)
    return top, narrow(x - widen(top))


def gather_pivots(device_count, place_ref, got_ref):
    panels, pivot_count = place_ref.shape
    parts = []
    for panel in range(panels):
        for half in range(pivot_count // lanes):
            place = place_ref[panel : panel + 1, half * lanes : (half + 1) * lanes]
            owner = jnp.broadcast_to(lax.div(place, lanes), (group, lanes))
            lane = jnp.broadcast_to(place, (group, lanes)) - owner * lanes
            taken = jnp.zeros((group, lanes), jnp.float32)
            for d in range(device_count):
                taken = jnp.where(owner == d, jnp.take_along_axis(got_ref[d], lane, axis=1), taken)
            parts.append(taken)
    return jnp.concatenate(parts, axis=1)


def factor_kernel(
    device_count,
    place_ref,
    got_ref,
    points_ref,
    scales_ref,
    out_ref,
    res_ref,
    s_ref,
    right_ref,
    mean_ref,
    diag_ref,
    off_ref,
    x_ref,
    y_ref,
    inv_ref,
    weight_ref,
    z1_ref,
    z2_ref,
    feat_ref,
    k_top,
    k_low,
    c1_top,
    c1_low,
    c2_top,
    c2_low,
    square_ref,
    stage_ref,
    sems,
):
    panels, width = place_ref.shape
    row_count = points_ref.shape[1]
    total = panels * width
    windows = block // window
    tile = row_count // (2 * windows)
    scale = scale_column(scales_ref)

    scaled = gather_pivots(device_count, place_ref, got_ref) * scale
    left = narrow(features(scaled, True))
    right = narrow(features(scaled, False))
    right_ref[...] = right
    kernel = jnp.exp2(product(left, right, 0, 0))
    mean_ref[...] = jnp.broadcast_to(jnp.sum(kernel, axis=0, keepdims=True) * (1.0 / total), (group, total))
    s_ref[...] = jnp.where(iota((total, total), 0) == iota((total, total), 1), kernel + nugget, kernel)
    off_ref[1] = jnp.zeros((block, block), jnp.float32)

    def squares(new):
        parts = [new[:, q * lanes : (q + 1) * lanes] for q in range(width // lanes)]
        return tree_sum([p * p for p in parts])

    def first_task(rows):
        scaled = points_ref[:, rows] * scale
        left = narrow(features(scaled, True).T)
        feat_ref[rows, :] = left
        kernel = jnp.exp2(product(left, right_ref[:, : 2 * width])) - mean_ref[0:1, : 2 * width]
        k_top[rows, :], k_low[rows, :] = two_parts(kernel)

    def second_task(rows):
        top, low = k_top[rows, :width], k_low[rows, :width]
        a = jnp.concatenate([top, low, top], axis=1)
        new = product(a, weight_ref[...], 1, 1) + (shift_0)
        stage_ref[rows, :] = new
        square_ref[rows, :] = squares(new)
        kernel = widen(k_top[rows, width:]) + widen(k_low[rows, width:])
        c1_top[rows, :], c1_low[rows, :] = two_parts(kernel - product(a, z1_ref[...]) + shift_1)

    def third_task(rows):
        top, low = c1_top[rows, :], c1_low[rows, :]
        new = product(jnp.concatenate([top, low, top], axis=1), weight_ref[...], 1, 1)
        stage_ref[rows, :] = new
        square_ref[rows, :] = square_ref[rows, :] + squares(new)
        top, low = k_top[rows, :], k_low[rows, :]
        a = jnp.concatenate([top, low, top], axis=1)
        kernel = jnp.exp2(product(feat_ref[rows, :], right_ref[:, 2 * width :]))
        c2_top[rows, :], c2_low[rows, :] = two_parts(kernel - product(a, z2_ref[...]) - shift_2)

    def send(panel, rows):
        return pltpu.make_async_copy(
            stage_ref.at[rows, :],
            out_ref.at[rows, panel * width : (panel + 1) * width],
            sems.at[panel],
        )

    def span(at, size):
        return pl.ds(pl.multiple_of(at, size), size)

    at = lambda p: slice(p * width, (p + 1) * width)
    tasks = [first_task, second_task, third_task]
    for p in range(panels):
        one = slice(p * width, p * width + block)
        two = slice(p * width + block, (p + 1) * width)
        diag_ref[0] = s_ref[one, one]
        diag_ref[1] = s_ref[two, two]
        off_ref[0] = s_ref[one, two]

        @pl.loop(0, 2)
        def _(half, p=p):
            answer = []
            for w in factor_block(diag_ref[half], answer):
                tasks[p](span((half * windows + w) * tile, tile))
            x = jnp.concatenate(answer, axis=0)
            x_ref[half] = x
            y = product(x, off_ref[half], precision=high)
            y_ref[half] = y
            diag_ref[half + 1] = diag_ref[half + 1] - product(y, y, 0, 0, high)
            if p > 0:
                send(p - 1, span(half * (row_count // 2), row_count // 2)).start()

        if p > 0:
            send(p - 1, slice(0, row_count)).wait()
        x0, x1 = x_ref[0], x_ref[1]
        corner = product(x1, product(y_ref[0], x0, 0, 0, high), precision=high)
        inverse = jnp.concatenate(
            [
                jnp.concatenate([x0, jnp.zeros((block, block), jnp.float32)], axis=1),
                jnp.concatenate([-corner, x1], axis=1),
            ],
            axis=0,
        )
        top, low = two_parts(inverse)
        weight_ref[...] = jnp.concatenate([top, top, low], axis=1)
        if p == 0:
            inv_ref[...] = inverse
            shift_0 = product(mean_ref[:, at(0)], inverse, 1, 1, high)[0:1, :]
            y01 = product(inverse, s_ref[at(0), width:], precision=high)
            s_ref[at(1), width:] = s_ref[at(1), width:] - product(y01[:, :width], y01, 0, 0, high)
            s_ref[at(2), at(2)] = s_ref[at(2), at(2)] - product(y01[:, width:], y01[:, width:], 0, 0, high)
            z = product(inverse, y01[:, :width], 0, 0, high)
            top, low = two_parts(z)
            z1_ref[...] = jnp.concatenate([top, top, low], axis=0)
            shift_1 = (mean_ref[:, at(1)] - product(mean_ref[:, at(0)], z, precision=high))[0:1, :]
            s_ref[at(0), width:] = y01
        if p == 1:
            y12 = product(inverse, s_ref[at(1), at(2)], precision=high)
            s_ref[at(2), at(2)] = s_ref[at(2), at(2)] - product(y12, y12, 0, 0, high)
            zb = product(inverse, y12, 0, 0, high)
            rest = s_ref[at(0), at(2)] - product(s_ref[at(0), at(1)], zb, precision=high)
            z = jnp.concatenate([product(inv_ref[...], rest, 0, 0, high), zb], axis=0)
            top, low = two_parts(z)
            z2_ref[...] = jnp.concatenate([top, top, low], axis=0)
            shift_2 = product(mean_ref[:, : 2 * width], z, precision=high)[0:1, :]

    last = row_count // 8

    @pl.loop(0, row_count // last)
    def _(i):
        rows = span(i * last, last)
        top, low = c2_top[rows, :], c2_low[rows, :]
        new = product(jnp.concatenate([top, low, top], axis=1), weight_ref[...], 1, 1)
        stage_ref[rows, :] = new
        send(panels - 1, rows).start()
        total_square = square_ref[rows, :] + squares(new)
        res_ref[0:1, rows] = 1.0 - jnp.sum(total_square.T, axis=0, keepdims=True)

    send(panels - 1, slice(0, row_count)).wait()


def on_device(points, inv_scales, pivots):
    dim, row_count = points.shape
    panels, pivot_count = pivots.shape
    device_count = lax.axis_size("rows")
    slot_count = 4 * pivot_count // device_count
    total = panels * pivot_count
    assert dim == group and panels * slot_count <= lanes and panels == 3 and pivot_count == 2 * block
    f32, bf16 = jnp.float32, jnp.bfloat16
    shape = jax.ShapeDtypeStruct
    vmem = pl.BlockSpec(memory_space=pltpu.VMEM)
    smem = pl.BlockSpec(memory_space=pltpu.SMEM)

    send, place = pl.pallas_call(
        functools.partial(select_kernel, row_count, slot_count, device_count),
        out_shape=(shape((device_count, group, lanes), f32), shape((panels, pivot_count), jnp.int32)),
        in_specs=[vmem, vmem],
        out_specs=(vmem, vmem),
        compiler_params=pltpu.CompilerParams(vmem_limit_bytes=16 * 2**20),
        name="select",
    )(points, pivots)
    got = lax.all_to_all(send, "rows", 0, 0)
    width = pivot_count
    factor, residual = pl.pallas_call(
        functools.partial(factor_kernel, device_count),
        out_shape=(shape((row_count, total), f32), shape((1, row_count), f32)),
        in_specs=[vmem, vmem, vmem, smem],
        out_specs=(pl.BlockSpec(memory_space=pl.ANY), vmem),
        scratch_shapes=[
            pltpu.VMEM((total, total), f32),
            pltpu.VMEM((feature_rows, total), bf16),
            pltpu.VMEM((group, total), f32),
            pltpu.VMEM((3, block, block), f32),
            pltpu.VMEM((2, block, block), f32),
            pltpu.VMEM((2, block, block), f32),
            pltpu.VMEM((2, block, block), f32),
            pltpu.VMEM((width, width), f32),
            pltpu.VMEM((width, 3 * width), bf16),
            pltpu.VMEM((3 * width, width), bf16),
            pltpu.VMEM((6 * width, width), bf16),
            pltpu.VMEM((row_count, feature_rows), bf16),
            pltpu.VMEM((row_count, 2 * width), bf16),
            pltpu.VMEM((row_count, 2 * width), bf16),
            pltpu.VMEM((row_count, width), bf16),
            pltpu.VMEM((row_count, width), bf16),
            pltpu.VMEM((row_count, width), bf16),
            pltpu.VMEM((row_count, width), bf16),
            pltpu.VMEM((row_count, lanes), f32),
            pltpu.VMEM((row_count, width), f32),
            pltpu.SemaphoreType.DMA((panels,)),
        ],
        compiler_params=pltpu.CompilerParams(vmem_limit_bytes=60 * 2**20),
        name="factor",
    )(place, got, points, inv_scales)
    return factor, residual.reshape(row_count)


def solution(mesh):
    return jax.shard_map(
        on_device,
        mesh=mesh,
        in_specs=(P(None, "rows"), P(), P()),
        out_specs=(P("rows", None), P("rows")),
        check_vma=False,
    )
```

time: 86.9 us -> 70.4 us (0.81)
  Pallas kernels: 66.7 us -> 52.3 us
  local copies, waits for them, and re-layouts: 3.93 us -> 1.64 us
    pallas_call x2 -> x1, Pallas kernels: 66.2 us -> 51.8 us  [on_device(): pl.pallas_call(functools.partial(factor_kernel, device_count), out_shape=...]
    unnamed x10 -> x6, local copies, waits for them, and re-layouts: 3.93 us -> 1.64 us
where the time goes in v2:
time: 70.4 us; the launch traced here: 70.2 us
  Pallas kernels  52.3 us (74%)
  blocking collectives  15.4 us (22%)
  local copies, waits for them, and re-layouts  1.64 us (2%)
  between operations  0.82 us (1%)
    pallas_call x1, Pallas kernels, on_device(): pl.pallas_call(functools.partial(factor_kernel, device_count), out_shape=...  51.8 us
    all_to_all x1, blocking collectives, on_device(): got = lax.all_to_all(send, 'rows', 0, 0)  15.4 us
    unnamed x6, local copies, waits for them, and re-layouts  1.64 us

profile of v2, /device:TPU:0, one launch (start us, length us, event | category | flops | bytes accessed | tf_op | source)
XLA Modules:
  0.0 70.2 jit_solution(7795979002484665975)
XLA Ops:
  0.6 0.0 copy-start
  0.6 0.9 %copy-done = f32[8,8192]{1,0:T(8,128)S(1)} copy-done((f32[8,8192]{1,0:T(8,128)S(1)}, f32[8,8192]{1,0:T(8,128)}, u32[]{:S(2)}) %copy-start) | copy-done | bytes 262168
  1.6 0.0 copy-start.1
  1.6 0.7 copy-done.1
  2.3 0.5 select.1
  2.8 0.0 copy-start.2
  2.8 15.4 %all_to_all.5.got_ref = f32[32,8,128]{2,1,0:T(8,128)} all-to-all(f32[32,8,128]{2,1,0:T(8,128)S(1)} %get-tuple-element.7), channel_id=1, replica_groups=mesh['rows'=32] {'rows'}, dimensions={0} | all-to-all | bytes 262144 | tf_op jit(solution)/shard_map/all_to_all | solution.py:383
  18.2 0.0 copy-done.2
  18.2 51.8 %factor.1 = (f32[8192,768]{1,0:T(8,128)}, f32[1,8192]{1,0:T(1,128)}) custom-call(s32[3,256]{1,0:T(4,128)} %copy-done.2, f32[32,8,128]{2,1,0:T(8,128)} %all_to_all.5.got_ref, f32[8,8192]{1,0:T(8,128)} %points_ref.3, f32[8]{0:T(128)} %scales_ref.1), custom_call_target="tpu_custom_call" | custom-call | tf_op jit(solution)/shard_map/factor/pallas_call | solution.py:385
Async XLA Ops:
  0.6 1.0 %copy-start = (f32[8,8192]{1,0:T(8,128)S(1)}, f32[8,8192]{1,0:T(8,128)}, u32[]{:S(2)}) copy-start(f32[8,8192]{1,0:T(8,128)} %points_ref.3) | copy-start | bytes 786436
  1.6 0.7 copy-start.1
  2.8 15.5 %copy-start.2 = (s32[3,256]{1,0:T(4,128)}, s32[3,256]{1,0:T(4,128)S(1)}, u32[]{:S(2)}) copy-start(s32[3,256]{1,0:T(4,128)S(1)} %get-tuple-element.6.place_ref) | copy-start | bytes 9220

commit v3 on v2

--- a/solution.py
+++ b/solution.py
@@ -13,6 +13,9 @@
 lanes = 128
 block = 128
 window = 16
+ahead = 1
+last_tiles = 4
+plan = (2, 2, 2, 2, 2, 2, 2, 0, 0, 0)
 feature_rows = 64
 high = lax.Precision.HIGHEST
 
@@ -39,7 +42,14 @@
     return x.astype(jnp.bfloat16)
 
 
-def select_kernel(row_count, slot_count, device_count, points_ref, pivots_ref, send_ref, place_ref):
+def select_kernel(
+    row_count, slot_count, device_count, points_hbm, pivots_hbm, send_ref, place_ref, points_ref, pivots_ref, sems
+):
+    pivots_in = pltpu.make_async_copy(pivots_hbm, pivots_ref, sems.at[0])
+    points_in = pltpu.make_async_copy(points_hbm, points_ref, sems.at[1])
+    pivots_in.start()
+    points_in.start()
+    pivots_in.wait()
     panels, pivot_count = pivots_ref.shape
     me = lax.axis_index("rows")
     before = narrow(
@@ -73,6 +83,7 @@
     found = product(values, chosen, 1, 1).astype(jnp.int32)
     tile = jnp.broadcast_to(found[0:1, :], (group, lanes))
     lane = jnp.broadcast_to(found[1:2, :], (group, lanes))
+    points_in.wait()
     taken = jnp.zeros((group, lanes), jnp.float32)
     for t in range(row_count // lanes):
         here = jnp.take_along_axis(points_ref[:, t * lanes : (t + 1) * lanes], lane, axis=1)
@@ -146,9 +157,12 @@
     for w in range(windows):
         first = w * window
         near = [column(rows[w], first + k) for k in range(window)]
-        after = [column(rows[w + 1], first + k) for k in range(window)] if w + 1 < windows else []
-        if w + 2 < windows:
-            left = narrow(stack_left(rows[w]).T)[(w + 2) * window :, :]
+        soon = range(w + 1, min(w + 1 + ahead, windows))
+        after = [[column(rows[v], first + k) for k in range(window)] for v in soon]
+        later = range(w + 1 + ahead, windows)
+        if later:
+            begin = later[0] * window // 16 * 16
+            left = narrow(stack_left(rows[w])).T[begin:, :]
         row_s, row_x, forward = rows[w], inv[w], inv[w]
         diag = None
         for j in range(0, window, 2):
@@ -171,16 +185,25 @@
             if j + 2 < window:
                 forward = forward - f2 * spread(forward, j + 1)
         answer.append(forward * lax.rsqrt(diag))
-        if w + 1 < windows:
-            rows[w + 1] = rows[w + 1] - tree_sum([after[k] * spread(row_s, k) for k in range(window)])
-            inv[w + 1] = inv[w + 1] - tree_sum([after[k] * spread(row_x, k) for k in range(window)])
-        if w + 2 < windows:
+        for v, cols in zip(soon, after):
+            rows[v] = rows[v] - tree_sum([cols[k] * spread(row_s, k) for k in range(window)])
+            inv[v] = inv[v] - tree_sum([cols[k] * spread(row_x, k) for k in range(window)])
+        if later:
             change = product(left, stack_right(jnp.concatenate([row_s, row_x], axis=1)))
-            for v in range(w + 2, windows):
-                at = (v - w - 2) * window
+            for v in later:
+                at = v * window - begin
                 rows[v] = rows[v] - change[at : at + window, :block]
                 inv[v] = inv[v] - change[at : at + window, block:]
         yield w
+
+
+def exact_product(a, b, a_dim=1, b_dim=0):
+    top, mid, low = (narrow(part) for part in split3(a))
+    if a_dim == 0:
+        top, mid, low = top.T, mid.T, low.T
+    left = jnp.concatenate([top, top, mid, top, low, mid], axis=1)
+    top, mid, low = (narrow(part) for part in split3(b))
+    return product(left, jnp.concatenate([top, mid, top, low, top, mid], axis=b_dim), 1, b_dim)
 
 
 def two_parts(x):
@@ -220,6 +243,7 @@
     y_ref,
     inv_ref,
     weight_ref,
+    shift_ref,
     z1_ref,
     z2_ref,
     feat_ref,
@@ -237,7 +261,7 @@
     row_count = points_ref.shape[1]
     total = panels * width
     windows = block // window
-    tile = row_count // (2 * windows)
+    tile = row_count // 32
     scale = scale_column(scales_ref)
 
     scaled = gather_pivots(device_count, place_ref, got_ref) * scale
@@ -255,7 +279,7 @@
 
     def first_task(rows):
         scaled = points_ref[:, rows] * scale
-        left = narrow(features(scaled, True).T)
+        left = narrow(features(scaled, True)).T
         feat_ref[rows, :] = left
         kernel = jnp.exp2(product(left, right_ref[:, : 2 * width])) - mean_ref[0:1, : 2 * width]
         k_top[rows, :], k_low[rows, :] = two_parts(kernel)
@@ -263,31 +287,45 @@
     def second_task(rows):
         top, low = k_top[rows, :width], k_low[rows, :width]
         a = jnp.concatenate([top, low, top], axis=1)
-        new = product(a, weight_ref[...], 1, 1) + (shift_0)
+        new = product(a, weight_ref[0], 1, 1) + shift_ref[0, 0:1, :]
         stage_ref[rows, :] = new
         square_ref[rows, :] = squares(new)
         kernel = widen(k_top[rows, width:]) + widen(k_low[rows, width:])
-        c1_top[rows, :], c1_low[rows, :] = two_parts(kernel - product(a, z1_ref[...]) + shift_1)
+        c1_top[rows, :], c1_low[rows, :] = two_parts(kernel - product(a, z1_ref[...]) + shift_ref[1, 0:1, :])
 
     def third_task(rows):
         top, low = c1_top[rows, :], c1_low[rows, :]
-        new = product(jnp.concatenate([top, low, top], axis=1), weight_ref[...], 1, 1)
+        new = product(jnp.concatenate([top, low, top], axis=1), weight_ref[1], 1, 1)
         stage_ref[rows, :] = new
         square_ref[rows, :] = square_ref[rows, :] + squares(new)
         top, low = k_top[rows, :], k_low[rows, :]
         a = jnp.concatenate([top, low, top], axis=1)
         kernel = jnp.exp2(product(feat_ref[rows, :], right_ref[:, 2 * width :]))
-        c2_top[rows, :], c2_low[rows, :] = two_parts(kernel - product(a, z2_ref[...]) - shift_2)
-
-    def send(panel, rows):
+        c2_top[rows, :], c2_low[rows, :] = two_parts(kernel - product(a, z2_ref[...]) - shift_ref[2, 0:1, :])
+
+    def last_task(rows):
+        top, low = c2_top[rows, :], c2_low[rows, :]
+        new = product(jnp.concatenate([top, low, top], axis=1), weight_ref[2], 1, 1)
+        stage_ref[rows, :] = new
+        total_square = square_ref[rows, :] + squares(new)
+        res_ref[0:1, rows] = 1.0 - jnp.sum(total_square.T, axis=0, keepdims=True)
+
+    def send(panel, part, rows):
         return pltpu.make_async_copy(
             stage_ref.at[rows, :],
             out_ref.at[rows, panel * width : (panel + 1) * width],
-            sems.at[panel],
+            sems.at[panel, part],
         )
 
     def span(at, size):
-        return pl.ds(pl.multiple_of(at, size), size)
+        return pl.ds(pl.multiple_of(at, tile), size)
+
+    tiles = row_count // tile
+    each = (tiles - last_tiles) // 2
+    part_rows = [(0, each * tile), (each * tile, each * tile), (2 * each * tile, last_tiles * tile)]
+
+    def wait(panel, part):
+        send(panel, part, pl.ds(*part_rows[part])).wait()
 
     at = lambda p: slice(p * width, (p + 1) * width)
     tasks = [first_task, second_task, third_task]
@@ -300,21 +338,33 @@
 
         @pl.loop(0, 2)
         def _(half, p=p):
+            given = []
+
+            def work(count):
+                for _ in range(count):
+                    tasks[p](span((half * each + len(given)) * tile, tile))
+                    given.append(0)
+
             answer = []
             for w in factor_block(diag_ref[half], answer):
-                tasks[p](span((half * windows + w) * tile, tile))
+                work(plan[w])
             x = jnp.concatenate(answer, axis=0)
             x_ref[half] = x
-            y = product(x, off_ref[half], precision=high)
+            y = exact_product(x, off_ref[half])
+            work(plan[windows])
             y_ref[half] = y
-            diag_ref[half + 1] = diag_ref[half + 1] - product(y, y, 0, 0, high)
+            diag_ref[half + 1] = diag_ref[half + 1] - exact_product(y, y, 0, 0)
+            work(plan[windows + 1])
+            assert len(given) == each
             if p > 0:
-                send(p - 1, span(half * (row_count // 2), row_count // 2)).start()
-
-        if p > 0:
-            send(p - 1, slice(0, row_count)).wait()
+                send(p - 1, half, span(half * (each * tile), each * tile)).start()
+
+        rest = [functools.partial(tasks[p], pl.ds((2 * each + i) * tile, tile)) for i in range(last_tiles)]
         x0, x1 = x_ref[0], x_ref[1]
-        corner = product(x1, product(y_ref[0], x0, 0, 0, high), precision=high)
+        corner = exact_product(x1, exact_product(y_ref[0], x0, 0, 0))
+        if p > 1:
+            wait(p - 2, 2)
+        rest.pop(0)()
         inverse = jnp.concatenate(
             [
                 jnp.concatenate([x0, jnp.zeros((block, block), jnp.float32)], axis=1),
@@ -323,41 +373,52 @@
             axis=0,
         )
         top, low = two_parts(inverse)
-        weight_ref[...] = jnp.concatenate([top, top, low], axis=1)
+        weight_ref[p] = jnp.concatenate([top, top, low], axis=1)
         if p == 0:
             inv_ref[...] = inverse
-            shift_0 = product(mean_ref[:, at(0)], inverse, 1, 1, high)[0:1, :]
-            y01 = product(inverse, s_ref[at(0), width:], precision=high)
-            s_ref[at(1), width:] = s_ref[at(1), width:] - product(y01[:, :width], y01, 0, 0, high)
-            s_ref[at(2), at(2)] = s_ref[at(2), at(2)] - product(y01[:, width:], y01[:, width:], 0, 0, high)
-            z = product(inverse, y01[:, :width], 0, 0, high)
+            shift_ref[0] = product(mean_ref[:, at(0)], inverse, 1, 1, high)
+            y01 = exact_product(inverse, s_ref[at(0), width:])
+            rest.pop(0)()
+            s_ref[at(1), width:] = s_ref[at(1), width:] - exact_product(y01[:, :width], y01, 0, 0)
+            s_ref[at(2), at(2)] = s_ref[at(2), at(2)] - exact_product(y01[:, width:], y01[:, width:], 0, 0)
+            z = exact_product(inverse, y01[:, :width], 0, 0)
             top, low = two_parts(z)
             z1_ref[...] = jnp.concatenate([top, top, low], axis=0)
-            shift_1 = (mean_ref[:, at(1)] - product(mean_ref[:, at(0)], z, precision=high))[0:1, :]
+            shift_ref[1] = mean_ref[:, at(1)] - product(mean_ref[:, at(0)], z, precision=high)
             s_ref[at(0), width:] = y01
         if p == 1:
-            y12 = product(inverse, s_ref[at(1), at(2)], precision=high)
-            s_ref[at(2), at(2)] = s_ref[at(2), at(2)] - product(y12, y12, 0, 0, high)
-            zb = product(inverse, y12, 0, 0, high)
-            rest = s_ref[at(0), at(2)] - product(s_ref[at(0), at(1)], zb, precision=high)
-            z = jnp.concatenate([product(inv_ref[...], rest, 0, 0, high), zb], axis=0)
+            y12 = exact_product(inverse, s_ref[at(1), at(2)])
+            rest.pop(0)()
+            s_ref[at(2), at(2)] = s_ref[at(2), at(2)] - exact_product(y12, y12, 0, 0)
+            zb = exact_product(inverse, y12, 0, 0)
+            far = s_ref[at(0), at(2)] - exact_product(s_ref[at(0), at(1)], zb)
+            z = jnp.concatenate([exact_product(inv_ref[...], far, 0, 0), zb], axis=0)
             top, low = two_parts(z)
             z2_ref[...] = jnp.concatenate([top, top, low], axis=0)
-            shift_2 = product(mean_ref[:, : 2 * width], z, precision=high)[0:1, :]
-
-    last = row_count // 8
-
-    @pl.loop(0, row_count // last)
-    def _(i):
-        rows = span(i * last, last)
-        top, low = c2_top[rows, :], c2_low[rows, :]
-        new = product(jnp.concatenate([top, low, top], axis=1), weight_ref[...], 1, 1)
-        stage_ref[rows, :] = new
-        send(panels - 1, rows).start()
-        total_square = square_ref[rows, :] + squares(new)
-        res_ref[0:1, rows] = 1.0 - jnp.sum(total_square.T, axis=0, keepdims=True)
-
-    send(panels - 1, slice(0, row_count)).wait()
+            shift_ref[2] = product(mean_ref[:, : 2 * width], z, precision=high)
+        for task in rest:
+            task()
+        if p == 1:
+            wait(0, 0)
+            wait(0, 1)
+        if p > 0:
+            send(p - 1, 2, pl.ds(*part_rows[2])).start()
+
+    pending = []
+    for part, (start, size) in enumerate(part_rows):
+        wait(panels - 2, part)
+        done = start
+        while done < start + size:
+            now = min(2 * tile, start + size - done)
+            last_task(pl.ds(done, now))
+            pending.append(send(panels - 1, part, pl.ds(done, now)))
+            done += now
+            if len(pending) > 2:
+                pending.pop(0).start()
+    for copy in pending:
+        copy.start()
+    for part in range(3):
+        wait(panels - 1, part)
 
 
 def on_device(points, inv_scales, pivots):
@@ -371,12 +432,18 @@
     shape = jax.ShapeDtypeStruct
     vmem = pl.BlockSpec(memory_space=pltpu.VMEM)
     smem = pl.BlockSpec(memory_space=pltpu.SMEM)
+    anywhere = pl.BlockSpec(memory_space=pltpu.HBM)
 
     send, place = pl.pallas_call(
         functools.partial(select_kernel, row_count, slot_count, device_count),
         out_shape=(shape((device_count, group, lanes), f32), shape((panels, pivot_count), jnp.int32)),
-        in_specs=[vmem, vmem],
+        in_specs=[anywhere, anywhere],
         out_specs=(vmem, vmem),
+        scratch_shapes=[
+            pltpu.VMEM((dim, row_count), f32),
+            pltpu.VMEM((panels, pivot_count), jnp.int32),
+            pltpu.SemaphoreType.DMA((2,)),
+        ],
         compiler_params=pltpu.CompilerParams(vmem_limit_bytes=16 * 2**20),
         name="select",
     )(points, pivots)
@@ -396,7 +463,8 @@
             pltpu.VMEM((2, block, block), f32),
             pltpu.VMEM((2, block, block), f32),
             pltpu.VMEM((width, width), f32),
-            pltpu.VMEM((width, 3 * width), bf16),
+            pltpu.VMEM((panels, width, 3 * width), bf16),
+            pltpu.VMEM((panels, group, width), f32),
             pltpu.VMEM((3 * width, width), bf16),
             pltpu.VMEM((6 * width, width), bf16),
             pltpu.VMEM((row_count, feature_rows), bf16),
@@ -408,7 +476,7 @@
             pltpu.VMEM((row_count, width), bf16),
             pltpu.VMEM((row_count, lanes), f32),
             pltpu.VMEM((row_count, width), f32),
-            pltpu.SemaphoreType.DMA((panels,)),
+            pltpu.SemaphoreType.DMA((panels, 3)),
         ],
         compiler_params=pltpu.CompilerParams(vmem_limit_bytes=60 * 2**20),
         name="factor",

time: 70.4 us -> 65.6 us (0.932)
  Pallas kernels: 52.3 us -> 47.5 us
    pallas_call x1, Pallas kernels: 51.8 us -> 47 us  [on_device(): pl.pallas_call(functools.partial(factor_kernel, device_count), out_shape=...]
where the time goes in v3:
time: 65.6 us; the launch traced here: 65.4 us
  Pallas kernels  47.5 us (72%)
  blocking collectives  15.4 us (23%)
  local copies, waits for them, and re-layouts  1.64 us (2%)
  between operations  0.84 us (1%)
    pallas_call x1, Pallas kernels, on_device(): pl.pallas_call(functools.partial(factor_kernel, device_count), out_shape=...  47 us
    all_to_all x1, blocking collectives, on_device(): got = lax.all_to_all(send, 'rows', 0, 0)  15.4 us
    unnamed x6, local copies, waits for them, and re-layouts  1.64 us

profile of v3, /device:TPU:0, one launch (start us, length us, event | category | flops | bytes accessed | tf_op | source)
XLA Modules:
  0.0 65.4 jit_solution(16845400258945640583)
XLA Ops:
  0.6 0.0 copy-start
  0.6 0.9 %copy-done = f32[8,8192]{1,0:T(8,128)S(1)} copy-done((f32[8,8192]{1,0:T(8,128)S(1)}, f32[8,8192]{1,0:T(8,128)}, u32[]{:S(2)}) %copy-start) | copy-done | bytes 262168
  1.6 0.0 copy-start.1
  1.6 0.7 %copy-done.1 = s32[3,256]{1,0:T(4,128)S(1)} copy-done((s32[3,256]{1,0:T(4,128)S(1)}, s32[3,256]{1,0:T(4,128)}, u32[]{:S(2)}) %copy-start.1) | copy-done | bytes 3096
  2.3 0.6 select.1
  2.8 0.0 copy-start.2
  2.8 15.4 %all_to_all.5.got_ref = f32[32,8,128]{2,1,0:T(8,128)} all-to-all(f32[32,8,128]{2,1,0:T(8,128)S(1)} %get-tuple-element.7), channel_id=1, replica_groups=mesh['rows'=32] {'rows'}, dimensions={0} | all-to-all | bytes 262144 | tf_op jit(solution)/shard_map/all_to_all | solution.py:450
  18.3 0.0 copy-done.2
  18.3 47.0 %factor.1 = (f32[8192,768]{1,0:T(8,128)}, f32[1,8192]{1,0:T(1,128)}) custom-call(s32[3,256]{1,0:T(4,128)} %copy-done.2, f32[32,8,128]{2,1,0:T(8,128)} %all_to_all.5.got_ref, f32[8,8192]{1,0:T(8,128)} %points_ref.1, f32[8]{0:T(128)} %scales_ref.1), custom_call_target="tpu_custom_call" | custom-call | tf_op jit(solution)/shard_map/factor/pallas_call | solution.py:452
Async XLA Ops:
  0.6 1.0 %copy-start = (f32[8,8192]{1,0:T(8,128)S(1)}, f32[8,8192]{1,0:T(8,128)}, u32[]{:S(2)}) copy-start(f32[8,8192]{1,0:T(8,128)} %points_ref.1) | copy-start | bytes 786436
  1.6 0.7 %copy-start.1 = (s32[3,256]{1,0:T(4,128)S(1)}, s32[3,256]{1,0:T(4,128)}, u32[]{:S(2)}) copy-start(s32[3,256]{1,0:T(4,128)} %pivots_hbm.1) | copy-start | bytes 9220
  2.8 15.5 %copy-start.2 = (s32[3,256]{1,0:T(4,128)}, s32[3,256]{1,0:T(4,128)S(1)}, u32[]{:S(2)}) copy-start(s32[3,256]{1,0:T(4,128)S(1)} %get-tuple-element.6.place_ref) | copy-start | bytes 9220

commit v4 on v3

--- a/solution.py
+++ b/solution.py
@@ -14,8 +14,8 @@
 block = 128
 window = 16
 ahead = 1
-last_tiles = 4
-plan = (2, 2, 2, 2, 2, 2, 2, 0, 0, 0)
+last_tiles = 8
+plan = (2, 2, 2, 2, 2, 1, 1, 0, 0, 0)
 feature_rows = 64
 high = lax.Precision.HIGHEST
 
@@ -365,6 +365,7 @@
         if p > 1:
             wait(p - 2, 2)
         rest.pop(0)()
+        rest.pop(0)()
         inverse = jnp.concatenate(
             [
                 jnp.concatenate([x0, jnp.zeros((block, block), jnp.float32)], axis=1),
@@ -379,8 +380,11 @@
             shift_ref[0] = product(mean_ref[:, at(0)], inverse, 1, 1, high)
             y01 = exact_product(inverse, s_ref[at(0), width:])
             rest.pop(0)()
+            rest.pop(0)()
             s_ref[at(1), width:] = s_ref[at(1), width:] - exact_product(y01[:, :width], y01, 0, 0)
             s_ref[at(2), at(2)] = s_ref[at(2), at(2)] - exact_product(y01[:, width:], y01[:, width:], 0, 0)
+            rest.pop(0)()
+            rest.pop(0)()
             z = exact_product(inverse, y01[:, :width], 0, 0)
             top, low = two_parts(z)
             z1_ref[...] = jnp.concatenate([top, top, low], axis=0)
@@ -389,8 +393,11 @@
         if p == 1:
             y12 = exact_product(inverse, s_ref[at(1), at(2)])
             rest.pop(0)()
+            rest.pop(0)()
             s_ref[at(2), at(2)] = s_ref[at(2), at(2)] - exact_product(y12, y12, 0, 0)
             zb = exact_product(inverse, y12, 0, 0)
+            rest.pop(0)()
+            rest.pop(0)()
             far = s_ref[at(0), at(2)] - exact_product(s_ref[at(0), at(1)], zb)
             z = jnp.concatenate([exact_product(inv_ref[...], far, 0, 0), zb], axis=0)
             top, low = two_parts(z)
@@ -444,7 +451,7 @@
             pltpu.VMEM((panels, pivot_count), jnp.int32),
             pltpu.SemaphoreType.DMA((2,)),
         ],
-        compiler_params=pltpu.CompilerParams(vmem_limit_bytes=16 * 2**20),
+        compiler_params=pltpu.CompilerParams(vmem_limit_bytes=60 * 2**20),
         name="select",
     )(points, pivots)
     got = lax.all_to_all(send, "rows", 0, 0)

time: 65.6 us -> 64.9 us (0.989)
  local copies, waits for them, and re-layouts: 1.64 us -> 0 us
  Pallas kernels: 47.5 us -> 48.2 us
    unnamed x6 -> x0, local copies, waits for them, and re-layouts: 1.64 us -> none
    pallas_call x1, Pallas kernels: 0.55 us -> 1.88 us  [on_device(): pl.pallas_call(functools.partial(select_kernel, row_count, slot_count, de...]
where the time goes in v4:
time: 64.9 us; the launch traced here: 64.7 us
  Pallas kernels  48.2 us (74%)
  blocking collectives  15.6 us (24%)
  between operations  0.82 us (1%)
    pallas_call x1, Pallas kernels, on_device(): pl.pallas_call(functools.partial(factor_kernel, device_count), out_shape=...  46.3 us
    all_to_all x1, blocking collectives, on_device(): got = lax.all_to_all(send, 'rows', 0, 0)  15.6 us
    pallas_call x1, Pallas kernels, on_device(): pl.pallas_call(functools.partial(select_kernel, row_count, slot_count, de...  1.88 us

profile of v4, /device:TPU:0, one launch (start us, length us, event | category | flops | bytes accessed | tf_op | source)
XLA Modules:
  0.0 64.7 jit_solution(17787345704304003384)
XLA Ops:
  0.6 1.9 %select.1 = (f32[32,8,128]{2,1,0:T(8,128)}, s32[3,256]{1,0:T(4,128)}) custom-call(f32[8,8192]{1,0:T(8,128)} %points_ref.1, s32[3,256]{1,0:T(4,128)} %pivots_hbm.1), custom_call_target="tpu_custom_call" | custom-call | tf_op jit(solution)/shard_map/select/pallas_call | solution.py:444
  2.5 15.6 %all_to_all.5.got_ref = f32[32,8,128]{2,1,0:T(8,128)} all-to-all(f32[32,8,128]{2,1,0:T(8,128)} %get-tuple-element.7), channel_id=1, replica_groups=mesh['rows'=32] {'rows'}, dimensions={0} | all-to-all | bytes 262144 | tf_op jit(solution)/shard_map/all_to_all | solution.py:457
  18.2 46.3 %factor.1 = (f32[8192,768]{1,0:T(8,128)}, f32[1,8192]{1,0:T(1,128)}) custom-call(s32[3,256]{1,0:T(4,128)} %get-tuple-element.6.place_ref, f32[32,8,128]{2,1,0:T(8,128)} %all_to_all.5.got_ref, f32[8,8192]{1,0:T(8,128)} %points_ref.1, f32[8]{0:T(128)} %scales_ref.1), custom_call_target="tpu_custom_call" | custom-call | tf_op jit(solution)/shard_map/factor/pallas_call | solution.py:459
